TPU v7x, 256 devices: a whole 4x4x8 slice. The times are simulated.
256 devices in a mesh: dp: 64 (over z_lo, y, x, core), tensor: 4 (over z_hi).
Axes of the slice: x: 4, y: 4, z: 8 (z_hi: 4, z_lo: 2; z = z_hi * 2 + z_lo), core: 2. Of those that a mesh axis runs over, the one named last changes fastest.
Arguments:
- acts: bfloat16 [8192, 8192], P('dp', 'tensor'), may hold values from -6 to 6
- gate_pre: bfloat16 [8192, 28672], P('dp', 'tensor'), may hold values from -8 to 8
- up_pre: bfloat16 [8192, 28672], P('dp', 'tensor'), may hold values from -6 to 6
- hidden_cot: bfloat16 [8192, 28672], P('dp', 'tensor'), may hold values from -6 to 6
- out_cot: bfloat16 [8192, 8192], P('dp', 'tensor'), may hold values from -6 to 6
- proj_model: bfloat16 [64, 8192], P(None, 'tensor'), may hold values from -0.0625 to 0.0625
- proj_hidden: bfloat16 [64, 28672], P(None, 'tensor'), may hold values from -0.03125 to 0.03125
- stored: bfloat16 [65024, 12288], P('dp', 'tensor'), may hold values from -6 to 6
- queries: bfloat16 [1024, 12288], P('dp', 'tensor'), may hold values from -0.0546875 to 0.0546875
- slots: int32 [512], P('dp'), may hold values from 0 to 511, as said below
Outputs:
- new_index: bfloat16 [512, 12288], P('dp', 'tensor')
- scores: float32 [65536, 1024], P(('dp', 'tensor'))
Inputs may be any that keep to these rules, and one draw needn't show every extreme that they name: slots is a permutation; entry e equals 8 times its owner block plus e % 8, and the 8 sequences of one dp index have different owner blocks.
All inputs are finite; a program needn't handle non-finite values.
Results may differ from a plain program's by a relative error of at most 0.014.
Values may be sent and summed in bfloat16 or wider, within the bound.
A program may use at most 128 MiB of HBM per device.

v0:
```python
import jax
import jax.numpy as jnp
from jax import lax
from jax.sharding import PartitionSpec as P

RANK = 64
SEQ_DEV = 8


def project(left, right):
    return lax.dot_general(
        left, right, (((1,), (1,)), ((), ())), preferred_element_type=jnp.float32
    )


def body(
    acts, gate_pre, up_pre, hidden_cot, out_cot, proj_model, proj_hidden, stored, queries, slots
):
    gate_float = gate_pre.astype(jnp.float32)
    up_float = up_pre.astype(jnp.float32)
    cot_float = hidden_cot.astype(jnp.float32)
    sigma = jax.nn.sigmoid(gate_float)
    silu_gate = gate_float * sigma
    hidden = (silu_gate * up_float).astype(jnp.bfloat16)
    up_cot = (cot_float * silu_gate).astype(jnp.bfloat16)
    gate_cot = (cot_float * up_float * sigma * (1.0 + gate_float * (1.0 - sigma))).astype(
        jnp.bfloat16
    )
    partial_sums = jnp.concatenate(
        [
            project(acts, proj_model),
            project(gate_cot, proj_hidden),
            project(up_cot, proj_hidden),
            project(hidden, proj_hidden),
            project(out_cot, proj_model),
        ],
        axis=1,
    )
    summed = lax.psum(partial_sums, "tensor")
    examples = SEQ_DEV
    window = summed.shape[0] // examples
    factors = summed.reshape(examples, window, 5, RANK)
    gate_grad = jnp.einsum("ewi,ewj->eij", factors[:, :, 0], factors[:, :, 1])
    up_grad = jnp.einsum("ewi,ewj->eij", factors[:, :, 0], factors[:, :, 2])
    down_grad = jnp.einsum("ewi,ewj->eij", factors[:, :, 3], factors[:, :, 4])
    gradients = jnp.concatenate(
        [
            gate_grad.reshape(examples, RANK * RANK),
            up_grad.reshape(examples, RANK * RANK),
            down_grad.reshape(examples, RANK * RANK),
        ],
        axis=1,
    )
    feat_width = stored.shape[1]
    own_rows = lax.dynamic_slice_in_dim(
        gradients, lax.axis_index("tensor") * feat_width, feat_width, 1
    ).astype(jnp.bfloat16)
    slot_ids = jnp.arange(examples, dtype=jnp.int32)
    first_slot = lax.axis_index("dp") * examples
    piece_rows = lax.all_gather(own_rows, "dp", axis=0, tiled=True)
    piece_slots = lax.all_gather(slots, "dp", axis=0, tiled=True)
    wanted = (piece_slots[None, :] == first_slot + slot_ids[:, None]).astype(jnp.bfloat16)
    new_block = jnp.dot(wanted, piece_rows, preferred_element_type=jnp.float32).astype(jnp.bfloat16)
    index_block = jnp.concatenate([stored, new_block], axis=0)
    query_panel = lax.all_gather(queries, "dp", axis=0, tiled=True)
    scores = lax.psum_scatter(
        project(index_block, query_panel), "tensor", scatter_dimension=0, tiled=True
    )
    return (new_block, scores)


def solution(mesh):
    return jax.shard_map(
        body,
        mesh=mesh,
        in_specs=(
            P("dp", "tensor"),
            P("dp", "tensor"),
            P("dp", "tensor"),
            P("dp", "tensor"),
            P("dp", "tensor"),
            P(None, "tensor"),
            P(None, "tensor"),
            P("dp", "tensor"),
            P("dp", "tensor"),
            P("dp"),
        ),
        out_specs=(P("dp", "tensor"), P(("dp", "tensor"), None)),
        check_vma=False,
    )
```

profile of v0, /device:TPU:1, one launch (start us, length us, event | category | flops | bytes accessed | tf_op | source)
XLA Modules:
  0.0 369.3 jit_solution(7665199801837896467)
XLA Ops:
  7.2 1.5 convolution_dynamic-update-slice_fusion.1
  8.7 4.5 %fusion.19 = f32[128,320]{0,1:T(8,128)S(1)} fusion(f32[128,320]{0,1:T(8,128)S(1)} %convolution_dynamic-update-slice_fusion.1, bf16[64,7168]{1,0:T(8,128)(2,1)S(1)} %copy-done, bf16[128,7168]{1,0:T(8,128)(2,1)} %param.12, bf16[128,7168]{1,0:T(8,128)(2,1)} %param.13, bf16[128,7168]{1,0:T(8,128)(2,1)} %param.11), kind=kOutput, calls=%fused_computation.25 | convolution fusion | flops 129368064 | bytes 6455296 | tf_op jit(solution)/shard_map/dot_general | solution.py:11
  13.3 1.3 fusion.22
  14.6 0.2 copy-done.5
  14.8 1.3 fusion.25
  16.1 0.3 convolution_dynamic-update-slice_fusion
  16.4 0.1 copy.13
  16.7 24.7 %all-reduce.2 = bf16[8,16,5,64]{3,1,0,2:T(8,128)(2,1)S(1)} all-reduce(f32[8,16,5,64]{3,1,0,2:T(8,128)S(1)} %copy.14), channel_id=1, replica_groups=mesh['dp'=64,'tensor'=4] {'tensor'}, use_global_device_ids=true, to_apply=%region_0.0 | all-reduce | flops 40960 | bytes 245760 | tf_op jit(solution)/shard_map/psum | solution.py:39
  41.4 0.2 fusion.32
  41.6 0.2 fusion.33
  41.9 0.2 fusion.31
  42.1 0.2 reshape.24
  42.3 0.2 reshape.23
  42.5 0.2 reshape.25
  42.6 0.9 fusion.30
  43.6 0.7 all-gather.5.cloned.1.call-update
  44.4 0.6 dynamic-slice
  45.7 0.2 dynamic-update-slice
  45.9 20.0 %all-reduce = s32[512]{0:T(512)S(1)} all-reduce(s32[512]{0:T(512)S(1)} %dynamic-update-slice), channel_id=1, replica_groups=mesh['dp'=64,'tensor'=4] {'dp'}, use_global_device_ids=true, to_apply=%add | all-reduce | flops 512 | bytes 4096
  65.9 90.0 %all-gather.3.cloned.1.call-done = bf16[512,3072]{1,0:T(8,128)(2,1)} async-done(((bf16[8,3072]{1,0:T(8,128)(2,1)}), bf16[512,3072]{1,0:T(8,128)(2,1)}) %all-gather.3.cloned.1.call-update) | async-done | bytes 3145744 | tf_op jit(solution)/shard_map/all_gather | solution.py:60
  155.9 2.4 convolution_convert_fusion
  158.3 109.4 %all-gather.5.cloned.1.call-done = bf16[1024,3072]{1,0:T(8,128)(2,1)} async-done(((bf16[16,3072]{1,0:T(8,128)(2,1)}), bf16[1024,3072]{1,0:T(8,128)(2,1)}) %all-gather.5.cloned.1.call-update) | async-done | bytes 6291472 | tf_op jit(solution)/shard_map/all_gather | solution.py:65
  267.8 12.0 %fusion = f32[1024,1024]{1,0:T(8,128)} fusion(bf16[1024,3072]{1,0:T(8,128)(2,1)} %all-gather.5.cloned.1.call-done, bf16[8,3072]{1,0:T(8,128)(2,1)S(1)} %convolution_convert_fusion, bf16[1016,3072]{1,0:T(8,128)(2,1)} %param.17), kind=kOutput, calls=%fused_computation | convolution fusion | flops 6455033856 | bytes 16777216 | tf_op jit(solution)/shard_map/dot_general | solution.py:11
  279.8 82.9 %reduce-scatter.2.cloned.1.call-done = f32[256,1024]{1,0:T(8,128)} async-done(((f32[1024,1024]{1,0:T(8,128)}), f32[256,1024]{1,0:T(8,128)}) %reduce-scatter.2.cloned.1.call-update) | async-done | bytes 1048592 | tf_op jit(solution)/shard_map/reduce_scatter | solution.py:66
  (26 shorter events, 0.4 us)
Async XLA Ops:
  7.2 1.5 copy-start
  7.2 148.7 %all-gather.3.cloned.1.call-start = ((), (), s32[]{:S(2)}) async-start(), calls=%async_computation.1 | async-start | bytes 3194880 | tf_op jit(solution)/shard_map/all_gather | solution.py:60
  8.7 4.5 %copy-start.4 = (bf16[128,7168]{1,0:T(8,128)(2,1)S(1)}, bf16[128,7168]{1,0:T(8,128)(2,1)}, u32[]{:S(2)}) copy-start(bf16[128,7168]{1,0:T(8,128)(2,1)} %param.13) | copy-start | bytes 5505028
  8.7 4.5 %copy-start.6 = (bf16[128,7168]{1,0:T(8,128)(2,1)S(1)}, bf16[128,7168]{1,0:T(8,128)(2,1)}, u32[]{:S(2)}) copy-start(bf16[128,7168]{1,0:T(8,128)(2,1)} %param.11) | copy-start | bytes 5505028
  13.3 1.5 copy-start.5
  14.8 1.3 copy-start.1
  14.8 1.3 copy-start.2
  16.1 28.3 %copy-start.8 = (u32[256]{0:T(256)S(1)}, u32[256]{0:T(256)}, u32[]{:S(2)}) copy-start(u32[256]{0:T(256)} %constant.24) | copy-start | bytes 3076
  16.1 29.6 %copy-start.7 = (s32[8]{0:T(128)S(1)}, s32[8]{0:T(128)}, u32[]{:S(2)}) copy-start(s32[8]{0:T(128)} %param.19) | copy-start | bytes 100
  43.6 224.2 %all-gather.5.cloned.1.call-start = ((), (), s32[]{:S(2)}) async-start(), calls=%async_computation.2 | async-start | bytes 6389760 | tf_op jit(solution)/shard_map/all_gather | solution.py:65
  44.3 318.4 %reduce-scatter.2.cloned.1.call-start = ((), (), s32[]{:S(2)}) async-start(), calls=%async_computation.3 | async-start | bytes 5242880 | tf_op jit(solution)/shard_map/reduce_scatter | solution.py:66
  158.3 121.5 %copy-start.3 = (bf16[8,3072]{1,0:T(8,128)(2,1)}, bf16[8,3072]{1,0:T(8,128)(2,1)S(1)}, u32[]{:S(2)}) copy-start(bf16[8,3072]{1,0:T(8,128)(2,1)S(1)} %convolution_convert_fusion) | copy-start | bytes 147460
Sparse Core Ops, SparseCore 0:
  43.7 112.1 all-gather.2
  157.7 109.9 all-gather.4
  279.9 82.7 reduce-scatter.1
where the time goes:
time: 369 us
  waiting for transfers between devices  283 us (77%)
  blocking collectives  44.6 us (12%)
  matrix products  24 us (7%)
  between operations  14.6 us (4%)
    all_gather x1, waiting for transfers between devices, body(): query_panel = lax.all_gather(queries, 'dp', axis=0, tiled=True)  109 us
    all_gather x1, waiting for transfers between devices, body(): piece_rows = lax.all_gather(own_rows, 'dp', axis=0, tiled=True)  90 us
    reduce_scatter x1, waiting for transfers between devices, body(): lax.psum_scatter(project(index_block, query_panel), 'tensor', scatter_dim...  82.9 us
    psum x1, blocking collectives, body(): summed = lax.psum(partial_sums, 'tensor')  24.7 us
    dot_general x6, matrix products, project(): lax.dot_general(left, right, (((1,), (1,)), ((), ())), preferred_element_...  20.9 us
    unnamed x1, blocking collectives  20 us
  transfers between devices with their start and end apart: 3, of which 3 were waited for; matrix products, arithmetic and copies ran while one was open for 1% of the time, Pallas kernels for 0%

commit v1 on v0

v1 whole, which is shorter than its diff:
```python
import jax
import jax.numpy as jnp
from jax import lax
from jax.experimental import pallas as pl
from jax.experimental.pallas import tpu as pltpu
from jax.sharding import PartitionSpec as P

MESH = pl.DeviceIdType.MESH
BF16, F32 = jnp.bfloat16, jnp.float32
RANK = 64
SHARD = 16
ROWS = 256
NQ = 1024
FEAT = 3072
HALF = FEAT // 2
PIECE = HALF + 128
TILE = 512
FLANES = 384


def product(left, right):
    return lax.dot_general(left, right, (((1,), (1,)), ((), ())), preferred_element_type=F32)


def iota(shape, dim):
    return lax.broadcasted_iota(jnp.int32, shape, dim)


class Place:
    def __init__(self):
        dp = lax.axis_index("dp")
        self.dp, self.t = dp, lax.axis_index("tensor")
        self.core = dp % 2
        self.x, self.y, self.zl = (dp // 2) % 4, (dp // 8) % 4, dp // 32
        self.a = self.x + self.core * (self.y - self.x)
        self.b = self.y + self.core * (self.x - self.y)

    def at(self, a, b, zl):
        x = a + self.core * (b - a)
        y = b + self.core * (a - b)
        return (((zl * 4 + y) * 4 + x) * 2 + self.core, self.t)

    def sibling(self):
        return (self.dp + 1 - 2 * self.core, self.t)

    def z_partner(self):
        return self.at(self.a, self.b, 1 - self.zl)

    def a_peer(self, k):
        return self.at((self.a + k) % 4, self.b, self.zl)

    def b_peer(self, k):
        return self.at(self.a, (self.b + k) % 4, self.zl)

    def tensor(self, k):
        return (self.dp, (self.t + k) % 4)


def slot(core, zl, b, a):
    return ((core * 2 + zl) * 4 + b) * 4 + a


class Gather:
    def __init__(self, me, panel, send, recv):
        self.me, self.panel, self.send, self.recv = me, panel, send, recv
        self.count = 0
        self.copies = []

    def copy(self, start, size, device):
        i = self.count
        self.count += 1
        part = self.panel.at[pl.ds(start, size)]
        made = pltpu.make_async_remote_copy(
            src_ref=part, dst_ref=part, send_sem=self.send.at[i], recv_sem=self.recv.at[i],
            device_id=device, device_id_type=MESH)
        made.start()
        self.copies.append(made)
        return made

    def own(self):
        me = self.me
        mine = slot(me.core, me.zl, me.b, me.a)
        self.sib0 = self.copy(mine, 1, me.sibling())
        self.a0 = [self.copy(mine, 1, me.a_peer(k)) for k in (1, 3, 2)]
        self.z = self.copy(mine, 1, me.z_partner())

    def after_z(self):
        me = self.me
        self.z.wait_recv()
        mine = slot(me.core, 1 - me.zl, me.b, me.a)
        self.a1 = [self.copy(mine, 1, me.a_peer(k)) for k in (1, 3, 2)]

    def after_a0(self):
        me = self.me
        self.sib_a0 = []
        for made, k in zip(self.a0, (1, 3, 2)):
            made.wait_recv()
            self.sib_a0.append(self.copy(slot(me.core, me.zl, me.b, (me.a + 4 - k) % 4), 1, me.sibling()))
        row = slot(me.core, me.zl, me.b, 0)
        self.b0 = [self.copy(row, 4, me.b_peer(k)) for k in (1, 3, 2)]

    def after_a1(self):
        me = self.me
        for made in self.a1:
            made.wait_recv()
        row = slot(me.core, 1 - me.zl, me.b, 0)
        self.sib_a1 = self.copy(row, 4, me.sibling())
        self.b1 = [self.copy(row, 4, me.b_peer(k)) for k in (1, 3, 2)]
        self.sib_b = {}

    def after_b(self, far, i):
        me = self.me
        k = (1, 3, 2)[i]
        (self.b1 if far else self.b0)[i].wait_recv()
        zl = 1 - me.zl if far else me.zl
        self.sib_b[far, i] = self.copy(slot(me.core, zl, (me.b + 4 - k) % 4, 0), 4, me.sibling())

    def finish(self):
        for made in self.copies:
            made.wait_send()


GATHER_COPIES = 1 + 3 + 1 + 3 + 3 + 3 + 1 + 3 + 6


def chunks(me):
    c, z, a, b = me.core, me.zl, me.a, me.b
    far = 1 - z
    result = [[(c, z, b, a, 1), (1 - c, z, a, b, 1)]]
    back = [3, 1, 2]
    result.append([(c, z, b, (a + k) % 4, 1) for k in back] + [(1 - c, z, a, (b + k) % 4, 1) for k in back])
    result.append([(c, far, b, 0, 4), (1 - c, far, a, 0, 4)])
    for zl in (z, far):
        for k in back:
            result.append([(c, zl, (b + k) % 4, 0, 4), (1 - c, zl, (a + k) % 4, 0, 4)])
    return result


CHUNK_ROWS = [32, 96] + [128] * 7
CHUNK_AT = [sum(CHUNK_ROWS[:i]) for i in range(len(CHUNK_ROWS))]
N_CHUNKS = len(CHUNK_ROWS)


def kernel(acts_hbm, gate_hbm, up_hbm, cot_hbm, outc_hbm, pm_hbm, ph_hbm, stored_hbm, queries_hbm, slots_ref,
           new_ref, out_ref,
           acts, gate, up, cot, outc, pm, ph, stored, panel, gpanel,
           acc, fac, fac_in, hsend, hrecv, g32,
           s1p, s1m, r1p, r1m, s2p, s2m, r2p, r2m, pp, pm_part, po, nsend, nrecv,
           local_sem, q_send, q_recv, g_send, g_recv, rs_send, rs_recv, f_send, f_recv, h_send, h_recv, n_send, n_recv):
    me = Place()
    t = me.t

    mine = slot(me.core, me.zl, me.b, me.a)
    own_q = pltpu.make_async_copy(queries_hbm, panel.at[mine], local_sem.at[0])
    own_q.start()
    stored_in = [
        pltpu.make_async_copy(stored_hbm.at[pl.ds(256 * i, 256 if i < 3 else 248)],
                              stored.at[pl.ds(256 * i, 256 if i < 3 else 248)], local_sem.at[1 + i])
        for i in range(4)
    ]
    stored[1008:, :] = jnp.zeros((16, FEAT), BF16)
    for made in stored_in:
        made.start()
    hidden_in = [pltpu.make_async_copy(src, dst, local_sem.at[5 + i]) for i, (src, dst) in enumerate(
        [(gate_hbm, gate), (up_hbm, up), (cot_hbm, cot), (ph_hbm, ph), (acts_hbm, acts), (outc_hbm, outc), (pm_hbm, pm)])]
    for made in hidden_in:
        made.start()

    barrier = pltpu.get_barrier_semaphore()
    partners = [me.sibling(), me.z_partner()]
    for k in (1, 2, 3):
        partners += [me.a_peer(k), me.b_peer(k), me.tensor(k)]
    for device in partners:
        pl.semaphore_signal(barrier, inc=1, device_id=device, device_id_type=MESH)
    pl.semaphore_wait(barrier, len(partners))

    gather = Gather(me, panel, q_send, q_recv)
    own_q.wait()
    gather.own()
    for made in stored_in:
        made.wait()

    parts = chunks(me)
    blocks = [(t + k) % 4 for k in range(4)]
    rs_copies = []

    def rs_copy(src, dst, rows, index, k):
        made = pltpu.make_async_remote_copy(
            src_ref=src.at[rows], dst_ref=dst.at[rows], send_sem=rs_send.at[index], recv_sem=rs_recv.at[index],
            device_id=me.tensor(k), device_id_type=MESH)
        made.start()
        rs_copies.append(made)
        return made

    def score(i, block):
        total = None
        for column in range(0, FEAT, TILE):
            left = jnp.concatenate(
                [panel[pl.ds(slot(c, zl, b, a), n), :, column:column + TILE].reshape(n * SHARD, TILE)
                 for c, zl, b, a, n in parts[i]], axis=0)
            right = stored[pl.ds(pl.multiple_of(block * ROWS, ROWS), ROWS), column:column + TILE]
            term = product(left, right)
            total = term if total is None else total + term
        return total

    first, second = {}, {}

    def stage1(i):
        rows = pl.ds(CHUNK_AT[i], CHUNK_ROWS[i])
        part = score(i, blocks[2]).astype(BF16)
        s1p[rows, :] = part[:, :128]
        s1m[rows, :] = part[:, 128:]
        first[i] = (rs_copy(s1p, r1p, rows, 4 * i, 1), rs_copy(s1m, r1m, rows, 4 * i + 1, 3))
        pp[rows, :] = score(i, blocks[1])
        pm_part[rows, :] = score(i, blocks[3])
        po[rows, :] = score(i, blocks[0])

    def stage2(i):
        rows = pl.ds(CHUNK_AT[i], CHUNK_ROWS[i])
        s2p[rows, 128:] = pp[rows, 128:].astype(BF16)
        s2m[rows, :128] = pm_part[rows, :128].astype(BF16)
        first[i][0].wait_recv()
        s2p[rows, :128] = (pp[rows, :128] + r1p[rows, :].astype(F32)).astype(BF16)
        plus = rs_copy(s2p, r2p, rows, 4 * i + 2, 1)
        first[i][1].wait_recv()
        s2m[rows, 128:] = (pm_part[rows, 128:] + r1m[rows, :].astype(F32)).astype(BF16)
        minus = rs_copy(s2m, r2m, rows, 4 * i + 3, 3)
        second[i] = (plus, minus)

    def stage3(i):
        for made in second[i]:
            made.wait_recv()
        at = CHUNK_AT[i]
        for c, zl, b, a, n in parts[i]:
            for j in range(n):
                rows = pl.ds(at, SHARD)
                value = po[rows, :] + r2p[rows, :].astype(F32) + r2m[rows, :].astype(F32)
                x = (a + j) + c * (b - (a + j))
                y = b + c * ((a + j) - b)
                place = ((zl * 4 + y) * 4 + x) * 2 + c
                out_ref[pl.ds(pl.multiple_of(place * SHARD, SHARD), SHARD), :] = value
                at += SHARD

    def factors_part(begin, end):
        def step(i, total):
            columns = pl.ds(pl.multiple_of(i * TILE, TILE), TILE)
            g = gate[:, columns].astype(F32)
            u = up[:, columns].astype(F32)
            c = cot[:, columns].astype(F32)
            s = jax.nn.sigmoid(g)
            silu = g * s
            hidden = (silu * u).astype(BF16)
            up_cot = (c * silu).astype(BF16)
            gate_cot = (c * u * s * (1.0 + g * (1.0 - s))).astype(BF16)
            return total + product(jnp.concatenate([gate_cot, up_cot, hidden], axis=0), ph[:, columns])

        acc[...] += lax.fori_loop(begin, end, step, jnp.zeros((384, RANK), F32))

    fac_copies, h_copies = [], []

    def factors_send():
        model = product(jnp.concatenate([acts[...], outc[...]], axis=0), pm[...]).astype(BF16)
        hidden = acc[...].astype(BF16)
        row, lane = iota((RANK, FLANES), 0), iota((RANK, FLANES), 1)
        split = (row % 2) * 32 + row // 2

        def spread(value, target):
            return jnp.dot(value, (lane == target).astype(F32).astype(BF16), preferred_element_type=F32)

        fac[...] = (spread(model[:128], split) + spread(hidden[256:], split + 64) + spread(hidden[:128], row + 128)
                    + spread(hidden[128:256], row + 192) + spread(model[128:], row + 256)).astype(BF16)
        for k in (1, 2, 3):
            made = pltpu.make_async_remote_copy(
                src_ref=fac.at[pl.ds(pl.multiple_of(32 * blocks[k], 32), 32)], dst_ref=fac_in.at[k - 1],
                send_sem=f_send.at[k - 1], recv_sem=f_recv.at[k - 1],
                device_id=me.tensor(k), device_id_type=MESH)
            made.start()
            fac_copies.append(made)

    def gradients():
        total = fac[pl.ds(pl.multiple_of(32 * t, 32), 32), :].astype(F32)
        for k in (1, 2, 3):
            fac_copies[k - 1].wait_recv()
            total += fac_in[k - 1].astype(F32)
        low = iota((32, 128), 1) < RANK
        both = []
        for s in range(2):
            one = total[16 * s:16 * s + 16]
            outer = lax.dot_general(one[:, :128], one[:, 128:], (((0,), (0,)), ((), ())),
                                    precision=lax.Precision.HIGHEST, preferred_element_type=F32)
            m_even, m_odd = outer[:32, :128], outer[32:64, :128]
            h_even, h_odd = outer[64:96, 128:], outer[96:, 128:]
            both.append(jnp.concatenate([
                jnp.where(low, m_even, pltpu.roll(m_odd, 64, 1)),
                jnp.where(low, pltpu.roll(m_even, 64, 1), m_odd),
                jnp.where(low, h_even, pltpu.roll(h_odd, 64, 1))], axis=0))
        for k in range(4):
            hsend[k] = jnp.concatenate([both[0][24 * k:24 * k + 24], both[1][24 * k:24 * k + 24]], axis=0).astype(BF16)
        for k in (1, 2, 3):
            made = pltpu.make_async_remote_copy(
                src_ref=hsend.at[blocks[k]], dst_ref=hrecv.at[k - 1], send_sem=h_send.at[k - 1],
                recv_sem=h_recv.at[k - 1], device_id=me.tensor(k), device_id_type=MESH)
            made.start()
            h_copies.append(made)

    def shard():
        g32[pl.ds(pl.multiple_of(48 * t, 48), 48), :] = hsend[t].astype(F32)
        for k in (1, 2, 3):
            h_copies[k - 1].wait_recv()
            g32[pl.ds(pl.multiple_of(48 * ((t + 4 - k) % 4), 48), 48), :] = hrecv[k - 1].astype(F32)
        for k in range(12):
            gpanel[mine, :, 128 * k:128 * k + 128] = jnp.concatenate(
                [g32[pl.ds(k, 8, stride=24), :], g32[pl.ds(k + 12, 8, stride=24), :]], axis=0).astype(BF16)
        sequence = iota((SHARD, 128), 0) % 8
        owner = jnp.zeros((SHARD, 128), F32)
        for j in range(8):
            owner = jnp.where(sequence == j, (slots_ref[j] // 8).astype(F32), owner)
        gpanel[mine, :, HALF:] = owner.astype(BF16)

    n_copies = []

    def new_rows():
        total = jnp.zeros((128, HALF), F32)
        shape = (256, 128)
        right_row = (iota(shape, 0) % SHARD) == iota(shape, 1)
        number = me.dp.astype(F32)
        for i in range(4):
            part = gpanel[pl.ds(16 * i, 16)].reshape(256, PIECE)
            owner = part[:, HALF:].astype(F32)
            pick = jnp.where(jnp.logical_and(right_row, owner == number), 1.0, 0.0).astype(BF16)
            total += lax.dot_general(pick, part[:, :HALF], (((0,), (0,)), ((), ())), preferred_element_type=F32)
        rows = jnp.concatenate([total[:8], total[8:16]], axis=1)
        new_ref[...] = rows.astype(BF16)
        left = jnp.concatenate([rows, rows], axis=0).astype(BF16)
        halves = []
        for c in range(2):
            halves.append(jnp.concatenate(
                [product(left, panel[pl.ds(32 * c + 8 * i, 8)].reshape(128, FEAT))[:8] for i in range(4)], axis=1))
        nsend[...] = jnp.concatenate(halves, axis=0).astype(BF16)
        for k in (1, 2, 3):
            n_copies.append(pltpu.make_async_remote_copy(
                src_ref=nsend, dst_ref=nrecv.at[k - 1], send_sem=n_send.at[k - 1],
                recv_sem=n_recv.at[k - 1], device_id=me.tensor(k), device_id_type=MESH))
        for k in (1, 2, 3):
            @pl.when((t + k) % 4 == 3)
            def _():
                n_copies[k - 1].start()

    def new_scores():
        @pl.when(t == 3)
        def _():
            for made in n_copies:
                made.wait_recv()
            total = nsend[...].astype(F32)
            for k in range(3):
                total += nrecv[k].astype(F32)
            for c in range(2):
                turned = jnp.transpose(jnp.concatenate(
                    [jnp.zeros((120, 512), F32), total[8 * c:8 * c + 8]], axis=0))
                for zl in range(2):
                    for b in range(4):
                        for a in range(4):
                            x, y = (a, b) if c == 0 else (b, a)
                            place = ((zl * 4 + y) * 4 + x) * 2 + c
                            at = ((zl * 4 + b) * 4 + a) * SHARD
                            out_ref[place * SHARD:(place + 1) * SHARD, 128:] += turned[at:at + SHARD]
        for k in (1, 2, 3):
            @pl.when((t + k) % 4 == 3)
            def _():
                n_copies[k - 1].wait_send()

    acc[...] = jnp.zeros_like(acc)
    grads = Gather(me, gpanel, g_send, g_recv)

    gather.sib0.wait_recv()
    stage1(0)
    gather.after_a0()
    gather.after_z()
    for made in gather.sib_a0:
        made.wait_recv()
    stage1(1)
    stage2(0)
    for made in hidden_in:
        made.wait()
    factors_part(0, 7)
    gather.after_a1()
    stage2(1)
    gather.sib_a1.wait_recv()
    stage1(2)
    factors_part(7, 14)
    factors_send()
    stage2(2)
    gather.after_b(False, 0)
    gather.after_b(False, 1)
    gather.sib_b[False, 0].wait_recv()
    stage1(3)
    gradients()
    gather.sib_b[False, 1].wait_recv()
    stage1(4)
    stage2(3)
    shard()
    grads.own()
    gather.after_b(False, 2)
    gather.sib_b[False, 2].wait_recv()
    stage1(5)
    stage2(4)
    grads.after_a0()
    grads.after_z()
    gather.after_b(True, 0)
    gather.sib_b[True, 0].wait_recv()
    stage1(6)
    stage2(5)
    gather.after_b(True, 1)
    gather.sib_b[True, 1].wait_recv()
    stage1(7)
    grads.after_a1()
    stage2(6)
    gather.after_b(True, 2)
    gather.sib_b[True, 2].wait_recv()
    stage1(8)
    stage2(7)
    stage3(0)
    stage3(1)
    for far in (False, True):
        for i in range(3):
            grads.after_b(far, i)
    stage3(2)
    stage2(8)
    grads.sib0.wait_recv()
    for made in grads.sib_a0:
        made.wait_recv()
    grads.sib_a1.wait_recv()
    for far in (False, True):
        for i in range(3):
            grads.sib_b[far, i].wait_recv()
    new_rows()
    for i in range(3, N_CHUNKS):
        stage3(i)
    new_scores()

    gather.finish()
    grads.finish()
    for made in rs_copies + fac_copies + h_copies:
        made.wait_send()


def body(acts, gate_pre, up_pre, hidden_cot, out_cot, proj_model, proj_hidden, stored, queries, slots):
    tokens, model = acts.shape
    hidden = gate_pre.shape[1]
    vmem = pltpu.VMEM
    dma = pltpu.SemaphoreType.DMA
    new_block, turned = pl.pallas_call(
        kernel,
        out_shape=(jax.ShapeDtypeStruct((8, FEAT), BF16), jax.ShapeDtypeStruct((NQ, ROWS), F32)),
        in_specs=[pl.BlockSpec(memory_space=pl.ANY)] * 9 + [pl.BlockSpec(memory_space=pltpu.SMEM)],
        out_specs=(pl.BlockSpec(memory_space=pltpu.VMEM), pl.BlockSpec(memory_space=pltpu.VMEM)),
        scratch_shapes=[
            vmem((tokens, model), BF16), vmem((tokens, hidden), BF16), vmem((tokens, hidden), BF16),
            vmem((tokens, hidden), BF16), vmem((tokens, model), BF16), vmem((RANK, model), BF16),
            vmem((RANK, hidden), BF16), vmem((4 * ROWS, FEAT), BF16), vmem((64, SHARD, FEAT), BF16),
            vmem((64, SHARD, PIECE), BF16),
            vmem((384, RANK), F32), vmem((128, FLANES), BF16), vmem((3, 32, FLANES), BF16),
            vmem((4, 48, 128), BF16), vmem((3, 48, 128), BF16), vmem((192, 128), F32),
            vmem((NQ, 128), BF16), vmem((NQ, 128), BF16), vmem((NQ, 128), BF16), vmem((NQ, 128), BF16),
            vmem((NQ, ROWS), BF16), vmem((NQ, ROWS), BF16), vmem((NQ, ROWS), BF16), vmem((NQ, ROWS), BF16),
            vmem((NQ, ROWS), F32), vmem((NQ, ROWS), F32), vmem((NQ, ROWS), F32),
            vmem((SHARD, 512), BF16), vmem((3, SHARD, 512), BF16),
            dma((12,)), dma((GATHER_COPIES,)), dma((GATHER_COPIES,)), dma((GATHER_COPIES,)), dma((GATHER_COPIES,)),
            dma((4 * N_CHUNKS,)), dma((4 * N_CHUNKS,)), dma((3,)), dma((3,)), dma((3,)), dma((3,)), dma((3,)), dma((3,)),
        ],
        compiler_params=pltpu.CompilerParams(
            collective_id=0, has_side_effects=True, vmem_limit_bytes=56 * 2**20),
    )(acts, gate_pre, up_pre, hidden_cot, out_cot, proj_model, proj_hidden, stored, queries, slots)
    return new_block, turned.T


def solution(mesh):
    return jax.shard_map(
        body,
        mesh=mesh,
        in_specs=(
            P("dp", "tensor"), P("dp", "tensor"), P("dp", "tensor"), P("dp", "tensor"), P("dp", "tensor"),
            P(None, "tensor"), P(None, "tensor"), P("dp", "tensor"), P("dp", "tensor"), P("dp"),
        ),
        out_specs=(P("dp", "tensor"), P(("dp", "tensor"), None)),
        check_vma=False,
    )
```

time: 369 us -> 77.2 us (0.21)
  waiting for transfers between devices: 283 us -> 0 us
  Pallas kernels: 0 us -> 73.3 us
  blocking collectives: 44.6 us -> 0 us
  matrix products: 24 us -> 0 us
  between operations: 14.6 us -> 0.65 us
    all_gather x2 -> x0, waiting for transfers between devices: 199 us -> none  [the longest x1 109 us: body(): query_panel = lax.all_gather(queries, 'dp', axis=0, tiled=True)]
    reduce_scatter x1 -> x0, waiting for transfers between devices: 82.9 us -> none  [body(): lax.psum_scatter(project(index_block, query_panel), 'tensor', scatter_dim...]
    pallas_call x0 -> x1, Pallas kernels: none -> 73.3 us  [body(): pl.pallas_call(kernel, out_shape=(jax.ShapeDtypeStruct((8, FEAT), BF16),...]
    psum x1 -> x0, blocking collectives: 24.7 us -> none  [body(): summed = lax.psum(partial_sums, 'tensor')]
    dot_general x10 -> x0, matrix products: 24 us -> none  [the longest x6 20.9 us: project(): lax.dot_general(left, right, (((1,), (1,)), ((), ())), preferred_element_...]
    unnamed x1 -> x0, blocking collectives: 20 us -> none
  transfers between devices with their start and end apart: 3 -> 0, of which waited for: 3 -> 0; matrix products, arithmetic and copies ran while one was open for 1% -> 0% of each run, Pallas kernels for 0% -> 0%
where the time goes in v1:
time: 77.2 us; the launch traced here: 77.1 us
  Pallas kernels  73.3 us (95%)
  local copies, waits for them, and re-layouts  3.17 us (4%)
    pallas_call x1, Pallas kernels, body(): pl.pallas_call(kernel, out_shape=(jax.ShapeDtypeStruct((8, FEAT), BF16),...  73.3 us
    unnamed x4, local copies, waits for them, and re-layouts  3.17 us

profile of v1, /device:TPU:1, one launch (start us, length us, event | category | flops | bytes accessed | tf_op | source)
XLA Modules:
  0.0 77.1 jit_solution(16495773558099454557)
XLA Ops:
  0.6 73.3 %shard_map.113 = (bf16[8,3072]{1,0:T(8,128)(2,1)}, f32[1024,256]{1,0:T(8,128)}) custom-call(bf16[128,2048]{1,0:T(8,128)(2,1)} %acts_hbm.1, bf16[128,7168]{1,0:T(8,128)(2,1)} %gate_hbm.1, bf16[128,7168]{1,0:T(8,128)(2,1)} %up_hbm.1, bf16[128,7168]{1,0:T(8,128)(2,1)} %cot_hbm.1, bf16[128,2048]{1,0:T(8,128)(2,1)} %outc_hbm.1, bf16[64,2048]{1,0:T(8,128)(2,1)} %pm_hbm.1, ...), custom_call_target="tpu_custom_call" | custom-call | tf_op jit(solution)/shard_map/pallas_call | solution.py:452
  74.0 0.0 copy-start
  74.0 2.5 %copy.12 = f32[256,1024]{1,0:T(8,128)} copy(f32[256,1024]{0,1:T(8,128)} %bitcast.1) | data formatting | bytes 2097152
  76.5 0.0 copy-done
  76.5 0.6 copy.14
Async XLA Ops:
  74.0 2.6 %copy-start = (bf16[8,3072]{1,0:T(8,128)(2,1)S(1)}, bf16[8,3072]{1,0:T(8,128)(2,1)}, u32[]{:S(2)}) copy-start(bf16[8,3072]{1,0:T(8,128)(2,1)} %get-tuple-element.10) | copy-start | bytes 147460

commit v2 on v1

--- a/solution.py
+++ b/solution.py
@@ -55,88 +55,105 @@
     def tensor(self, k):
         return (self.dp, (self.t + k) % 4)
 
-
-def slot(core, zl, b, a):
-    return ((core * 2 + zl) * 4 + b) * 4 + a
+    def queries_of(self, p, z, b, a):
+        core = self.core + p * (1 - 2 * self.core)
+        first, second = (self.a, self.b) if p == 0 else (self.b, self.a)
+        a_at, b_at, z_at = (first + a) % 4, (second + b) % 4, (self.zl + z) % 2
+        x = a_at + core * (b_at - a_at)
+        y = b_at + core * (a_at - b_at)
+        return ((z_at * 4 + y) * 4 + x) * 2 + core
+
+
+def slot(p, z, b, a):
+    return ((p * 2 + z) * 4 + b) * 4 + a
 
 
 class Gather:
     def __init__(self, me, panel, send, recv):
         self.me, self.panel, self.send, self.recv = me, panel, send, recv
         self.count = 0
-        self.copies = []
-
-    def copy(self, start, size, device):
+        self.copies, self.landing, self.landed = [], {}, set()
+
+    def copy(self, source, target, device, size=1):
         i = self.count
         self.count += 1
-        part = self.panel.at[pl.ds(start, size)]
         made = pltpu.make_async_remote_copy(
-            src_ref=part, dst_ref=part, send_sem=self.send.at[i], recv_sem=self.recv.at[i],
-            device_id=device, device_id_type=MESH)
+            src_ref=self.panel.at[pl.ds(slot(*source), size)], dst_ref=self.panel.at[pl.ds(slot(*target), size)],
+            send_sem=self.send.at[i], recv_sem=self.recv.at[i], device_id=device, device_id_type=MESH)
         made.start()
         self.copies.append(made)
-        return made
-
-    def own(self):
-        me = self.me
-        mine = slot(me.core, me.zl, me.b, me.a)
-        self.sib0 = self.copy(mine, 1, me.sibling())
-        self.a0 = [self.copy(mine, 1, me.a_peer(k)) for k in (1, 3, 2)]
-        self.z = self.copy(mine, 1, me.z_partner())
-
-    def after_z(self):
-        me = self.me
-        self.z.wait_recv()
-        mine = slot(me.core, 1 - me.zl, me.b, me.a)
-        self.a1 = [self.copy(mine, 1, me.a_peer(k)) for k in (1, 3, 2)]
-
-    def after_a0(self):
-        me = self.me
-        self.sib_a0 = []
-        for made, k in zip(self.a0, (1, 3, 2)):
-            made.wait_recv()
-            self.sib_a0.append(self.copy(slot(me.core, me.zl, me.b, (me.a + 4 - k) % 4), 1, me.sibling()))
-        row = slot(me.core, me.zl, me.b, 0)
-        self.b0 = [self.copy(row, 4, me.b_peer(k)) for k in (1, 3, 2)]
-
-    def after_a1(self):
-        me = self.me
-        for made in self.a1:
-            made.wait_recv()
-        row = slot(me.core, 1 - me.zl, me.b, 0)
-        self.sib_a1 = self.copy(row, 4, me.sibling())
-        self.b1 = [self.copy(row, 4, me.b_peer(k)) for k in (1, 3, 2)]
-        self.sib_b = {}
-
-    def after_b(self, far, i):
-        me = self.me
-        k = (1, 3, 2)[i]
-        (self.b1 if far else self.b0)[i].wait_recv()
-        zl = 1 - me.zl if far else me.zl
-        self.sib_b[far, i] = self.copy(slot(me.core, zl, (me.b + 4 - k) % 4, 0), 4, me.sibling())
+        for j in range(size):
+            self.landing[slot(*target) + j] = i
+
+    def wait(self, *places):
+        for place in places:
+            i = self.landing[slot(*place)]
+            if i not in self.landed:
+                self.landed.add(i)
+                self.copies[i].wait_recv()
+
+    def to_sibling(self, z, b, a, size=1):
+        self.copy((0, z, b, a), (1, z, b, a), self.me.sibling(), size)
+
+    def along_a(self, z, k):
+        self.copy((0, z, 0, 0), (0, z, 0, 4 - k), self.me.a_peer(k))
+
+    def along_b(self, z, a):
+        for k in (1, 3):
+            self.copy((0, z, 0, a), (0, z, 4 - k, a), self.me.b_peer(k))
+
+    def start(self):
+        self.to_sibling(0, 0, 0)
+        self.along_a(0, 1)
+        self.along_a(0, 3)
+        self.along_b(0, 0)
+        self.copy((0, 0, 0, 0), (0, 1, 0, 0), self.me.z_partner())
+        self.along_a(0, 2)
+
+    def on_z(self):
+        self.wait((0, 1, 0, 0))
+        self.along_a(1, 1)
+        self.along_a(1, 3)
+        self.along_b(1, 0)
+        self.along_a(1, 2)
+        self.to_sibling(1, 0, 0)
+
+    def on_a(self, z, a):
+        self.wait((0, z, 0, a))
+        self.along_b(z, a)
+        self.to_sibling(z, 0, a)
+
+    def on_b(self, z, a):
+        for b in (1, 3):
+            self.wait((0, z, b, a))
+            self.to_sibling(z, b, a)
+
+    def pass_on(self, z, low):
+        if low:
+            self.copy((0, z, 3, 0), (0, z, 2, 0), self.me.b_peer(1), 2)
+        else:
+            self.copy((0, z, 1, 2), (0, z, 2, 2), self.me.b_peer(3), 2)
+
+    def on_opposite(self, z):
+        self.wait((0, z, 2, 0), (0, z, 2, 2))
+        self.to_sibling(z, 2, 0, 4)
 
     def finish(self):
         for made in self.copies:
             made.wait_send()
 
 
-GATHER_COPIES = 1 + 3 + 1 + 3 + 3 + 3 + 1 + 3 + 6
-
-
-def chunks(me):
-    c, z, a, b = me.core, me.zl, me.a, me.b
-    far = 1 - z
-    result = [[(c, z, b, a, 1), (1 - c, z, a, b, 1)]]
-    back = [3, 1, 2]
-    result.append([(c, z, b, (a + k) % 4, 1) for k in back] + [(1 - c, z, a, (b + k) % 4, 1) for k in back])
-    result.append([(c, far, b, 0, 4), (1 - c, far, a, 0, 4)])
-    for zl in (z, far):
-        for k in back:
-            result.append([(c, zl, (b + k) % 4, 0, 4), (1 - c, zl, (a + k) % 4, 0, 4)])
-    return result
-
-
-CHUNK_ROWS = [32, 96] + [128] * 7
+GATHER_COPIES = 7 + 9 + 6 + 9 + 16 + 4 + 2
+
+CHUNKS = [
+    [(0, 0, 0, 0), (1, 0, 0, 0), (0, 0, 0, 1), (0, 0, 0, 3), (1, 0, 0, 1), (1, 0, 0, 3), (0, 0, 1, 0), (0, 0, 3, 0)],
+    [(0, 0, 0, 2), (1, 0, 0, 2), (0, 0, 1, 1), (0, 0, 3, 1), (0, 0, 1, 3), (0, 0, 3, 3), (1, 0, 1, 0), (1, 0, 3, 0)],
+    [(0, 1, 0, 0), (1, 1, 0, 0), (0, 1, 0, 1), (0, 1, 0, 3), (1, 1, 0, 1), (1, 1, 0, 3), (0, 0, 1, 2), (0, 0, 3, 2)],
+    [(1, 0, b, a) for b in (1, 3) for a in (1, 2, 3)] + [(0, 1, 0, 2), (1, 1, 0, 2), (0, 1, 1, 0), (0, 1, 3, 0)],
+    [(p, 0, 2, a) for p in (0, 1) for a in range(4)] + [(0, 1, b, a) for b in (1, 3) for a in (1, 2, 3)],
+    [(1, 1, b, a) for b in (1, 3) for a in range(4)] + [(p, 1, 2, a) for p in (0, 1) for a in range(4)],
+]
+CHUNK_ROWS = [SHARD * len(parts) for parts in CHUNKS]
 CHUNK_AT = [sum(CHUNK_ROWS[:i]) for i in range(len(CHUNK_ROWS))]
 N_CHUNKS = len(CHUNK_ROWS)
 
@@ -145,12 +162,12 @@
            new_ref, out_ref,
            acts, gate, up, cot, outc, pm, ph, stored, panel, gpanel,
            acc, fac, fac_in, hsend, hrecv, g32,
-           s1p, s1m, r1p, r1m, s2p, s2m, r2p, r2m, pp, pm_part, po, nsend, nrecv,
+           send, recv, pp, pm_part, po, nsend, nrecv,
            local_sem, q_send, q_recv, g_send, g_recv, rs_send, rs_recv, f_send, f_recv, h_send, h_recv, n_send, n_recv):
     me = Place()
     t = me.t
 
-    mine = slot(me.core, me.zl, me.b, me.a)
+    mine = 0
     own_q = pltpu.make_async_copy(queries_hbm, panel.at[mine], local_sem.at[0])
     own_q.start()
     stored_in = [
@@ -159,10 +176,9 @@
         for i in range(4)
     ]
     stored[1008:, :] = jnp.zeros((16, FEAT), BF16)
-    for made in stored_in:
-        made.start()
     hidden_in = [pltpu.make_async_copy(src, dst, local_sem.at[5 + i]) for i, (src, dst) in enumerate(
         [(gate_hbm, gate), (up_hbm, up), (cot_hbm, cot), (ph_hbm, ph), (acts_hbm, acts), (outc_hbm, outc), (pm_hbm, pm)])]
+
     for made in hidden_in:
         made.start()
 
@@ -176,70 +192,66 @@
 
     gather = Gather(me, panel, q_send, q_recv)
     own_q.wait()
-    gather.own()
-    for made in stored_in:
-        made.wait()
-
-    parts = chunks(me)
+    gather.start()
+
     blocks = [(t + k) % 4 for k in range(4)]
     rs_copies = []
 
-    def rs_copy(src, dst, rows, index, k):
+    def rs_copy(i, kind, k):
+        rows = pl.ds(CHUNK_AT[i], CHUNK_ROWS[i])
         made = pltpu.make_async_remote_copy(
-            src_ref=src.at[rows], dst_ref=dst.at[rows], send_sem=rs_send.at[index], recv_sem=rs_recv.at[index],
-            device_id=me.tensor(k), device_id_type=MESH)
+            src_ref=send.at[kind, rows], dst_ref=recv.at[kind, rows], send_sem=rs_send.at[6 * i + kind],
+            recv_sem=rs_recv.at[6 * i + kind], device_id=me.tensor(k), device_id_type=MESH)
         made.start()
         rs_copies.append(made)
-        return made
+        reduce[i, kind] = made
 
     def score(i, block):
         total = None
         for column in range(0, FEAT, TILE):
             left = jnp.concatenate(
-                [panel[pl.ds(slot(c, zl, b, a), n), :, column:column + TILE].reshape(n * SHARD, TILE)
-                 for c, zl, b, a, n in parts[i]], axis=0)
+                [panel[slot(*place), :, column:column + TILE] for place in CHUNKS[i]], axis=0)
             right = stored[pl.ds(pl.multiple_of(block * ROWS, ROWS), ROWS), column:column + TILE]
             term = product(left, right)
             total = term if total is None else total + term
         return total
 
-    first, second = {}, {}
+    reduce = {}
 
     def stage1(i):
         rows = pl.ds(CHUNK_AT[i], CHUNK_ROWS[i])
-        part = score(i, blocks[2]).astype(BF16)
-        s1p[rows, :] = part[:, :128]
-        s1m[rows, :] = part[:, 128:]
-        first[i] = (rs_copy(s1p, r1p, rows, 4 * i, 1), rs_copy(s1m, r1m, rows, 4 * i + 1, 3))
-        pp[rows, :] = score(i, blocks[1])
-        pm_part[rows, :] = score(i, blocks[3])
+        part = score(i, blocks[2])
+        send[0, rows, :] = part[:, :128].astype(BF16)
+        rs_copy(i, 0, 1)
+        send[1, rows, :] = part[:, 128:].astype(BF16)
+        rs_copy(i, 1, 3)
+        part = score(i, blocks[1])
+        send[2, rows, :] = part[:, 128:].astype(BF16)
+        rs_copy(i, 2, 1)
+        pp[rows, :] = part[:, :128]
+        part = score(i, blocks[3])
+        send[3, rows, :] = part[:, :128].astype(BF16)
+        rs_copy(i, 3, 3)
+        pm_part[rows, :] = part[:, 128:]
         po[rows, :] = score(i, blocks[0])
 
     def stage2(i):
         rows = pl.ds(CHUNK_AT[i], CHUNK_ROWS[i])
-        s2p[rows, 128:] = pp[rows, 128:].astype(BF16)
-        s2m[rows, :128] = pm_part[rows, :128].astype(BF16)
-        first[i][0].wait_recv()
-        s2p[rows, :128] = (pp[rows, :128] + r1p[rows, :].astype(F32)).astype(BF16)
-        plus = rs_copy(s2p, r2p, rows, 4 * i + 2, 1)
-        first[i][1].wait_recv()
-        s2m[rows, 128:] = (pm_part[rows, 128:] + r1m[rows, :].astype(F32)).astype(BF16)
-        minus = rs_copy(s2m, r2m, rows, 4 * i + 3, 3)
-        second[i] = (plus, minus)
+        reduce[i, 0].wait_recv()
+        send[4, rows, :] = (pp[rows, :] + recv[0, rows, :].astype(F32)).astype(BF16)
+        rs_copy(i, 4, 1)
+        reduce[i, 1].wait_recv()
+        send[5, rows, :] = (pm_part[rows, :] + recv[1, rows, :].astype(F32)).astype(BF16)
+        rs_copy(i, 5, 3)
 
     def stage3(i):
-        for made in second[i]:
-            made.wait_recv()
-        at = CHUNK_AT[i]
-        for c, zl, b, a, n in parts[i]:
-            for j in range(n):
-                rows = pl.ds(at, SHARD)
-                value = po[rows, :] + r2p[rows, :].astype(F32) + r2m[rows, :].astype(F32)
-                x = (a + j) + c * (b - (a + j))
-                y = b + c * ((a + j) - b)
-                place = ((zl * 4 + y) * 4 + x) * 2 + c
-                out_ref[pl.ds(pl.multiple_of(place * SHARD, SHARD), SHARD), :] = value
-                at += SHARD
+        for kind in (2, 3, 4, 5):
+            reduce[i, kind].wait_recv()
+        for j, place in enumerate(CHUNKS[i]):
+            rows = pl.ds(CHUNK_AT[i] + SHARD * j, SHARD)
+            target = pl.ds(pl.multiple_of(me.queries_of(*place) * SHARD, SHARD), SHARD)
+            out_ref[target, :128] = po[rows, :128] + recv[3, rows, :].astype(F32) + recv[4, rows, :].astype(F32)
+            out_ref[target, 128:] = po[rows, 128:] + recv[2, rows, :].astype(F32) + recv[5, rows, :].astype(F32)
 
     def factors_part(begin, end):
         def step(i, total):
@@ -357,13 +369,12 @@
             for c in range(2):
                 turned = jnp.transpose(jnp.concatenate(
                     [jnp.zeros((120, 512), F32), total[8 * c:8 * c + 8]], axis=0))
-                for zl in range(2):
+                for z in range(2):
                     for b in range(4):
                         for a in range(4):
-                            x, y = (a, b) if c == 0 else (b, a)
-                            place = ((zl * 4 + y) * 4 + x) * 2 + c
-                            at = ((zl * 4 + b) * 4 + a) * SHARD
-                            out_ref[place * SHARD:(place + 1) * SHARD, 128:] += turned[at:at + SHARD]
+                            target = pl.ds(pl.multiple_of(me.queries_of(c, z, b, a) * SHARD, SHARD), SHARD)
+                            at = slot(0, z, b, a) * SHARD
+                            out_ref[target, 128:] += turned[at:at + SHARD]
         for k in (1, 2, 3):
             @pl.when((t + k) % 4 == 3)
             def _():
@@ -372,70 +383,84 @@
     acc[...] = jnp.zeros_like(acc)
     grads = Gather(me, gpanel, g_send, g_recv)
 
-    gather.sib0.wait_recv()
-    stage1(0)
-    gather.after_a0()
-    gather.after_z()
-    for made in gather.sib_a0:
-        made.wait_recv()
-    stage1(1)
-    stage2(0)
+    def chunk(i):
+        gather.wait(*[place for place in CHUNKS[i] if place != (0, 0, 0, 0)])
+        stage1(i)
+
     for made in hidden_in:
         made.wait()
-    factors_part(0, 7)
-    gather.after_a1()
+    for made in stored_in:
+        made.start()
+    factors_part(0, 9)
+    gather.on_a(0, 1)
+    gather.on_a(0, 3)
+    gather.on_z()
+    gather.on_b(0, 0)
+    factors_part(9, 14)
+    factors_send()
+    gather.on_a(0, 2)
+    for made in stored_in:
+        made.wait()
+    chunk(0)
+    gather.on_b(0, 1)
+    gather.pass_on(0, True)
+    gather.on_b(0, 3)
+    gather.on_a(1, 1)
+    gather.on_a(1, 3)
+    chunk(1)
+    gather.on_b(0, 2)
+    gather.pass_on(0, False)
+    gather.on_a(1, 2)
+    gather.on_b(1, 0)
+    chunk(2)
+    stage2(0)
+    gradients()
+    gather.on_b(1, 1)
+    gather.pass_on(1, True)
+    gather.on_b(1, 3)
+    gather.on_opposite(0)
+    gather.on_b(1, 2)
+    gather.pass_on(1, False)
     stage2(1)
-    gather.sib_a1.wait_recv()
-    stage1(2)
-    factors_part(7, 14)
-    factors_send()
+    shard()
+    grads.start()
+    chunk(3)
+    gather.on_opposite(1)
     stage2(2)
-    gather.after_b(False, 0)
-    gather.after_b(False, 1)
-    gather.sib_b[False, 0].wait_recv()
-    stage1(3)
-    gradients()
-    gather.sib_b[False, 1].wait_recv()
-    stage1(4)
+    grads.on_a(0, 1)
+    grads.on_a(0, 3)
+    chunk(4)
+    grads.on_a(0, 2)
+    grads.on_z()
+    grads.on_b(0, 0)
+    chunk(5)
+    stage3(0)
+    grads.on_b(0, 1)
+    grads.pass_on(0, True)
+    grads.on_b(0, 3)
+    grads.on_b(0, 2)
+    grads.pass_on(0, False)
     stage2(3)
-    shard()
-    grads.own()
-    gather.after_b(False, 2)
-    gather.sib_b[False, 2].wait_recv()
-    stage1(5)
+    grads.on_a(1, 1)
+    grads.on_a(1, 3)
+    grads.on_a(1, 2)
+    grads.on_b(1, 0)
+    stage3(1)
     stage2(4)
-    grads.after_a0()
-    grads.after_z()
-    gather.after_b(True, 0)
-    gather.sib_b[True, 0].wait_recv()
-    stage1(6)
+    grads.on_opposite(0)
+    grads.on_b(1, 1)
+    grads.pass_on(1, True)
+    grads.on_b(1, 3)
+    grads.on_b(1, 2)
+    grads.pass_on(1, False)
+    stage3(2)
     stage2(5)
-    gather.after_b(True, 1)
-    gather.sib_b[True, 1].wait_recv()
-    stage1(7)
-    grads.after_a1()
-    stage2(6)
-    gather.after_b(True, 2)
-    gather.sib_b[True, 2].wait_recv()
-    stage1(8)
-    stage2(7)
-    stage3(0)
-    stage3(1)
-    for far in (False, True):
-        for i in range(3):
-            grads.after_b(far, i)
-    stage3(2)
-    stage2(8)
-    grads.sib0.wait_recv()
-    for made in grads.sib_a0:
-        made.wait_recv()
-    grads.sib_a1.wait_recv()
-    for far in (False, True):
-        for i in range(3):
-            grads.sib_b[far, i].wait_recv()
+    stage3(3)
+    grads.on_opposite(1)
+    grads.wait(*[(p, z, b, a) for p in range(2) for z in range(2) for b in range(4) for a in range(4) if p + z + b + a])
     new_rows()
-    for i in range(3, N_CHUNKS):
-        stage3(i)
+    stage3(4)
+    stage3(5)
     new_scores()
 
     gather.finish()
@@ -461,12 +486,11 @@
             vmem((64, SHARD, PIECE), BF16),
             vmem((384, RANK), F32), vmem((128, FLANES), BF16), vmem((3, 32, FLANES), BF16),
             vmem((4, 48, 128), BF16), vmem((3, 48, 128), BF16), vmem((192, 128), F32),
-            vmem((NQ, 128), BF16), vmem((NQ, 128), BF16), vmem((NQ, 128), BF16), vmem((NQ, 128), BF16),
-            vmem((NQ, ROWS), BF16), vmem((NQ, ROWS), BF16), vmem((NQ, ROWS), BF16), vmem((NQ, ROWS), BF16),
-            vmem((NQ, ROWS), F32), vmem((NQ, ROWS), F32), vmem((NQ, ROWS), F32),
+            vmem((6, NQ, 128), BF16), vmem((6, NQ, 128), BF16),
+            vmem((NQ, 128), F32), vmem((NQ, 128), F32), vmem((NQ, ROWS), F32),
             vmem((SHARD, 512), BF16), vmem((3, SHARD, 512), BF16),
             dma((12,)), dma((GATHER_COPIES,)), dma((GATHER_COPIES,)), dma((GATHER_COPIES,)), dma((GATHER_COPIES,)),
-            dma((4 * N_CHUNKS,)), dma((4 * N_CHUNKS,)), dma((3,)), dma((3,)), dma((3,)), dma((3,)), dma((3,)), dma((3,)),
+            dma((6 * N_CHUNKS,)), dma((6 * N_CHUNKS,)), dma((3,)), dma((3,)), dma((3,)), dma((3,)), dma((3,)), dma((3,)),
         ],
         compiler_params=pltpu.CompilerParams(
             collective_id=0, has_side_effects=True, vmem_limit_bytes=56 * 2**20),

time: 77.2 us -> 71.8 us (0.930); the launches traced: 77.1 us -> 70.6 us
  Pallas kernels: 73.3 us -> 66.7 us
    pallas_call x1, Pallas kernels: 73.3 us -> 66.7 us  [body(): pl.pallas_call(kernel, out_shape=(jax.ShapeDtypeStruct((8, FEAT), BF16),...]
where the time goes in v2:
time: 71.8 us; the launch traced here: 70.6 us
  Pallas kernels  66.7 us (93%)
  local copies, waits for them, and re-layouts  3.17 us (4%)
    pallas_call x1, Pallas kernels, body(): pl.pallas_call(kernel, out_shape=(jax.ShapeDtypeStruct((8, FEAT), BF16),...  66.7 us
    unnamed x4, local copies, waits for them, and re-layouts  3.17 us

profile of v2, /device:TPU:1, one launch (start us, length us, event | category | flops | bytes accessed | tf_op | source)
XLA Modules:
  0.0 70.6 jit_solution(15624245243930236865)
XLA Ops:
  0.6 66.7 %shard_map.113 = (bf16[8,3072]{1,0:T(8,128)(2,1)}, f32[1024,256]{1,0:T(8,128)}) custom-call(bf16[128,2048]{1,0:T(8,128)(2,1)} %acts_hbm.1, bf16[128,7168]{1,0:T(8,128)(2,1)} %gate_hbm.1, bf16[128,7168]{1,0:T(8,128)(2,1)} %up_hbm.1, bf16[128,7168]{1,0:T(8,128)(2,1)} %cot_hbm.1, bf16[128,2048]{1,0:T(8,128)(2,1)} %outc_hbm.1, bf16[64,2048]{1,0:T(8,128)(2,1)} %pm_hbm.1, ...), custom_call_target="tpu_custom_call" | custom-call | tf_op jit(solution)/shard_map/pallas_call | solution.py:477
  67.4 0.0 copy-start
  67.4 2.5 %copy.12 = f32[256,1024]{1,0:T(8,128)} copy(f32[256,1024]{0,1:T(8,128)} %bitcast.1) | data formatting | bytes 2097152
  69.9 0.0 copy-done
  69.9 0.6 copy.14
Async XLA Ops:
  67.4 2.6 %copy-start = (bf16[8,3072]{1,0:T(8,128)(2,1)S(1)}, bf16[8,3072]{1,0:T(8,128)(2,1)}, u32[]{:S(2)}) copy-start(bf16[8,3072]{1,0:T(8,128)(2,1)} %get-tuple-element.10) | copy-start | bytes 147460

commit v3 on v2

--- a/solution.py
+++ b/solution.py
@@ -161,7 +161,7 @@
 def kernel(acts_hbm, gate_hbm, up_hbm, cot_hbm, outc_hbm, pm_hbm, ph_hbm, stored_hbm, queries_hbm, slots_ref,
            new_ref, out_ref,
            acts, gate, up, cot, outc, pm, ph, stored, panel, gpanel,
-           acc, fac, fac_in, hsend, hrecv, g32,
+           acc, chosen, fac, fac_in, hsend, hrecv, g32,
            send, recv, pp, pm_part, po, nsend, nrecv,
            local_sem, q_send, q_recv, g_send, g_recv, rs_send, rs_recv, f_send, f_recv, h_send, h_recv, n_send, n_recv):
     me = Place()
@@ -259,16 +259,16 @@
             g = gate[:, columns].astype(F32)
             u = up[:, columns].astype(F32)
             c = cot[:, columns].astype(F32)
-            s = jax.nn.sigmoid(g)
+            s = 0.5 * jnp.tanh(0.5 * g) + 0.5
             silu = g * s
             hidden = (silu * u).astype(BF16)
             up_cot = (c * silu).astype(BF16)
-            gate_cot = (c * u * s * (1.0 + g * (1.0 - s))).astype(BF16)
+            gate_cot = (c * u * (s + silu * (1.0 - s))).astype(BF16)
             return total + product(jnp.concatenate([gate_cot, up_cot, hidden], axis=0), ph[:, columns])
 
         acc[...] += lax.fori_loop(begin, end, step, jnp.zeros((384, RANK), F32))
 
-    fac_copies, h_copies = [], []
+    fac_copies, h_copies = {}, {}
 
     def factors_send():
         model = product(jnp.concatenate([acts[...], outc[...]], axis=0), pm[...]).astype(BF16)
@@ -281,18 +281,18 @@
 
         fac[...] = (spread(model[:128], split) + spread(hidden[256:], split + 64) + spread(hidden[:128], row + 128)
                     + spread(hidden[128:256], row + 192) + spread(model[128:], row + 256)).astype(BF16)
-        for k in (1, 2, 3):
+        for k in (2, 1, 3):
             made = pltpu.make_async_remote_copy(
                 src_ref=fac.at[pl.ds(pl.multiple_of(32 * blocks[k], 32), 32)], dst_ref=fac_in.at[k - 1],
                 send_sem=f_send.at[k - 1], recv_sem=f_recv.at[k - 1],
                 device_id=me.tensor(k), device_id_type=MESH)
             made.start()
-            fac_copies.append(made)
+            fac_copies[k] = made
 
     def gradients():
         total = fac[pl.ds(pl.multiple_of(32 * t, 32), 32), :].astype(F32)
         for k in (1, 2, 3):
-            fac_copies[k - 1].wait_recv()
+            fac_copies[k].wait_recv()
             total += fac_in[k - 1].astype(F32)
         low = iota((32, 128), 1) < RANK
         both = []
@@ -308,17 +308,17 @@
                 jnp.where(low, h_even, pltpu.roll(h_odd, 64, 1))], axis=0))
         for k in range(4):
             hsend[k] = jnp.concatenate([both[0][24 * k:24 * k + 24], both[1][24 * k:24 * k + 24]], axis=0).astype(BF16)
-        for k in (1, 2, 3):
+        for k in (2, 1, 3):
             made = pltpu.make_async_remote_copy(
                 src_ref=hsend.at[blocks[k]], dst_ref=hrecv.at[k - 1], send_sem=h_send.at[k - 1],
                 recv_sem=h_recv.at[k - 1], device_id=me.tensor(k), device_id_type=MESH)
             made.start()
-            h_copies.append(made)
+            h_copies[k] = made
 
     def shard():
         g32[pl.ds(pl.multiple_of(48 * t, 48), 48), :] = hsend[t].astype(F32)
         for k in (1, 2, 3):
-            h_copies[k - 1].wait_recv()
+            h_copies[k].wait_recv()
             g32[pl.ds(pl.multiple_of(48 * ((t + 4 - k) % 4), 48), 48), :] = hrecv[k - 1].astype(F32)
         for k in range(12):
             gpanel[mine, :, 128 * k:128 * k + 128] = jnp.concatenate(
@@ -331,16 +331,20 @@
 
     n_copies = []
 
-    def new_rows():
-        total = jnp.zeros((128, HALF), F32)
+    def pick(part):
         shape = (256, 128)
         right_row = (iota(shape, 0) % SHARD) == iota(shape, 1)
-        number = me.dp.astype(F32)
-        for i in range(4):
-            part = gpanel[pl.ds(16 * i, 16)].reshape(256, PIECE)
-            owner = part[:, HALF:].astype(F32)
-            pick = jnp.where(jnp.logical_and(right_row, owner == number), 1.0, 0.0).astype(BF16)
-            total += lax.dot_general(pick, part[:, :HALF], (((0,), (0,)), ((), ())), preferred_element_type=F32)
+        owner = part[:, HALF:].astype(F32)
+        chosen = jnp.where(jnp.logical_and(right_row, owner == me.dp.astype(F32)), 1.0, 0.0).astype(BF16)
+        return lax.dot_general(chosen, part[:, :HALF], (((0,), (0,)), ((), ())), preferred_element_type=F32)[:SHARD]
+
+    def picked(z):
+        grads.wait(*[(p, z, b, a) for p in range(2) for b in range(4) for a in range(4) if p + z + b + a])
+        chosen[...] += pick(gpanel[pl.ds(slot(0, z, 0, 0), 16)].reshape(256, PIECE))
+        chosen[...] += pick(gpanel[pl.ds(slot(1, z, 0, 0), 16)].reshape(256, PIECE))
+
+    def new_rows():
+        total = chosen[...]
         rows = jnp.concatenate([total[:8], total[8:16]], axis=1)
         new_ref[...] = rows.astype(BF16)
         left = jnp.concatenate([rows, rows], axis=0).astype(BF16)
@@ -369,18 +373,18 @@
             for c in range(2):
                 turned = jnp.transpose(jnp.concatenate(
                     [jnp.zeros((120, 512), F32), total[8 * c:8 * c + 8]], axis=0))
-                for z in range(2):
-                    for b in range(4):
-                        for a in range(4):
-                            target = pl.ds(pl.multiple_of(me.queries_of(c, z, b, a) * SHARD, SHARD), SHARD)
-                            at = slot(0, z, b, a) * SHARD
-                            out_ref[target, 128:] += turned[at:at + SHARD]
+                for i, parts in enumerate(CHUNKS):
+                    for j, place in enumerate(parts):
+                        if place[0] == c:
+                            at = slot(0, *place[1:]) * SHARD
+                            po[pl.ds(CHUNK_AT[i] + SHARD * j, SHARD), 128:] += turned[at:at + SHARD]
         for k in (1, 2, 3):
             @pl.when((t + k) % 4 == 3)
             def _():
                 n_copies[k - 1].wait_send()
 
     acc[...] = jnp.zeros_like(acc)
+    chosen[...] = jnp.zeros_like(chosen)
     grads = Gather(me, gpanel, g_send, g_recv)
 
     def chunk(i):
@@ -391,30 +395,29 @@
         made.wait()
     for made in stored_in:
         made.start()
-    factors_part(0, 9)
+    factors_part(0, 14)
     gather.on_a(0, 1)
     gather.on_a(0, 3)
+    factors_send()
     gather.on_z()
     gather.on_b(0, 0)
-    factors_part(9, 14)
-    factors_send()
-    gather.on_a(0, 2)
     for made in stored_in:
         made.wait()
     chunk(0)
+    gather.on_a(0, 2)
     gather.on_b(0, 1)
     gather.pass_on(0, True)
     gather.on_b(0, 3)
     gather.on_a(1, 1)
     gather.on_a(1, 3)
     chunk(1)
+    gradients()
     gather.on_b(0, 2)
     gather.pass_on(0, False)
     gather.on_a(1, 2)
     gather.on_b(1, 0)
+    stage2(0)
     chunk(2)
-    stage2(0)
-    gradients()
     gather.on_b(1, 1)
     gather.pass_on(1, True)
     gather.on_b(1, 3)
@@ -426,47 +429,50 @@
     grads.start()
     chunk(3)
     gather.on_opposite(1)
-    stage2(2)
     grads.on_a(0, 1)
     grads.on_a(0, 3)
+    grads.on_z()
+    grads.on_a(0, 2)
+    grads.on_b(0, 0)
+    stage2(2)
     chunk(4)
-    grads.on_a(0, 2)
-    grads.on_z()
-    grads.on_b(0, 0)
-    chunk(5)
-    stage3(0)
     grads.on_b(0, 1)
     grads.pass_on(0, True)
     grads.on_b(0, 3)
-    grads.on_b(0, 2)
-    grads.pass_on(0, False)
-    stage2(3)
     grads.on_a(1, 1)
     grads.on_a(1, 3)
     grads.on_a(1, 2)
+    grads.on_b(0, 2)
+    grads.pass_on(0, False)
     grads.on_b(1, 0)
-    stage3(1)
-    stage2(4)
-    grads.on_opposite(0)
+    chunk(5)
     grads.on_b(1, 1)
     grads.pass_on(1, True)
     grads.on_b(1, 3)
     grads.on_b(1, 2)
     grads.pass_on(1, False)
-    stage3(2)
+    stage2(3)
+    grads.on_opposite(0)
+    stage2(4)
+    picked(0)
     stage2(5)
-    stage3(3)
     grads.on_opposite(1)
-    grads.wait(*[(p, z, b, a) for p in range(2) for z in range(2) for b in range(4) for a in range(4) if p + z + b + a])
+    picked(1)
     new_rows()
-    stage3(4)
-    stage3(5)
     new_scores()
+    for i in range(N_CHUNKS):
+        stage3(i)
+
 
     gather.finish()
     grads.finish()
-    for made in rs_copies + fac_copies + h_copies:
+    for made in rs_copies + list(fac_copies.values()) + list(h_copies.values()):
         made.wait_send()
+
+
+def finish(rows_ref, turned_ref, new_ref, scores_ref):
+    new_ref[...] = rows_ref[...]
+    scores_ref[...] = turned_ref[...].T
 
 
 def body(acts, gate_pre, up_pre, hidden_cot, out_cot, proj_model, proj_hidden, stored, queries, slots):
@@ -484,7 +490,7 @@
             vmem((tokens, hidden), BF16), vmem((tokens, model), BF16), vmem((RANK, model), BF16),
             vmem((RANK, hidden), BF16), vmem((4 * ROWS, FEAT), BF16), vmem((64, SHARD, FEAT), BF16),
             vmem((64, SHARD, PIECE), BF16),
-            vmem((384, RANK), F32), vmem((128, FLANES), BF16), vmem((3, 32, FLANES), BF16),
+            vmem((384, RANK), F32), vmem((SHARD, HALF), F32), vmem((128, FLANES), BF16), vmem((3, 32, FLANES), BF16),
             vmem((4, 48, 128), BF16), vmem((3, 48, 128), BF16), vmem((192, 128), F32),
             vmem((6, NQ, 128), BF16), vmem((6, NQ, 128), BF16),
             vmem((NQ, 128), F32), vmem((NQ, 128), F32), vmem((NQ, ROWS), F32),
@@ -495,7 +501,10 @@
         compiler_params=pltpu.CompilerParams(
             collective_id=0, has_side_effects=True, vmem_limit_bytes=56 * 2**20),
     )(acts, gate_pre, up_pre, hidden_cot, out_cot, proj_model, proj_hidden, stored, queries, slots)
-    return new_block, turned.T
+    return pl.pallas_call(
+        finish,
+        out_shape=(jax.ShapeDtypeStruct((8, FEAT), BF16), jax.ShapeDtypeStruct((ROWS, NQ), F32)),
+    )(new_block, turned)
 
 
 def solution(mesh):

time: 71.8 us -> 66.6 us (0.928); the launches traced: 70.6 us -> 66.5 us
  local copies, waits for them, and re-layouts: 3.17 us -> 0 us
  Pallas kernels: 66.7 us -> 65.9 us
    pallas_call x1, Pallas kernels: 66.7 us -> 63.3 us  [body(): pl.pallas_call(kernel, out_shape=(jax.ShapeDtypeStruct((8, FEAT), BF16),...]
    unnamed x4 -> x0, local copies, waits for them, and re-layouts: 3.17 us -> none
    pallas_call x0 -> x1, Pallas kernels: none -> 2.56 us  [body(): pl.pallas_call(finish, out_shape=(jax.ShapeDtypeStruct((8, FEAT), BF16),...]
where the time goes in v3:
time: 66.6 us; the launch traced here: 66.5 us
  Pallas kernels  65.9 us (99%)
    pallas_call x1, Pallas kernels, body(): pl.pallas_call(kernel, out_shape=(jax.ShapeDtypeStruct((8, FEAT), BF16),...  63.3 us
    pallas_call x1, Pallas kernels, body(): pl.pallas_call(finish, out_shape=(jax.ShapeDtypeStruct((8, FEAT), BF16),...  2.56 us

profile of v3, /device:TPU:1, one launch (start us, length us, event | category | flops | bytes accessed | tf_op | source)
XLA Modules:
  0.0 66.5 jit_solution(9906390092491441015)
XLA Ops:
  0.6 63.3 %shard_map.113 = (bf16[8,3072]{1,0:T(8,128)(2,1)}, f32[1024,256]{1,0:T(8,128)}) custom-call(bf16[128,2048]{1,0:T(8,128)(2,1)} %acts_hbm.1, bf16[128,7168]{1,0:T(8,128)(2,1)} %gate_hbm.1, bf16[128,7168]{1,0:T(8,128)(2,1)} %up_hbm.1, bf16[128,7168]{1,0:T(8,128)(2,1)} %cot_hbm.1, bf16[128,2048]{1,0:T(8,128)(2,1)} %outc_hbm.1, bf16[64,2048]{1,0:T(8,128)(2,1)} %pm_hbm.1, ...), custom_call_target="tpu_custom_call" | custom-call | tf_op jit(solution)/shard_map/pallas_call | solution.py:483
  63.9 2.6 %shard_map.114 = (bf16[8,3072]{1,0:T(8,128)(2,1)}, f32[256,1024]{1,0:T(8,128)}) custom-call(bf16[8,3072]{1,0:T(8,128)(2,1)} %get-tuple-element.4.rows_ref, f32[1024,256]{1,0:T(8,128)} %get-tuple-element.5.turned_ref), custom_call_target="tpu_custom_call" | custom-call | tf_op jit(solution)/shard_map/pallas_call | solution.py:504

commit v4 on v3

--- a/solution.py
+++ b/solution.py
@@ -424,9 +424,9 @@
     gather.on_opposite(0)
     gather.on_b(1, 2)
     gather.pass_on(1, False)
-    stage2(1)
     shard()
     grads.start()
+    stage2(1)
     chunk(3)
     gather.on_opposite(1)
     grads.on_a(0, 1)
@@ -455,8 +455,8 @@
     grads.on_opposite(0)
     stage2(4)
     picked(0)
+    grads.on_opposite(1)
     stage2(5)
-    grads.on_opposite(1)
     picked(1)
     new_rows()
     new_scores()
@@ -482,7 +482,7 @@
     dma = pltpu.SemaphoreType.DMA
     new_block, turned = pl.pallas_call(
         kernel,
-        out_shape=(jax.ShapeDtypeStruct((8, FEAT), BF16), jax.ShapeDtypeStruct((NQ, ROWS), F32)),
+        out_shape=(pltpu.VMEM((8, FEAT), BF16), pltpu.VMEM((NQ, ROWS), F32)),
         in_specs=[pl.BlockSpec(memory_space=pl.ANY)] * 9 + [pl.BlockSpec(memory_space=pltpu.SMEM)],
         out_specs=(pl.BlockSpec(memory_space=pltpu.VMEM), pl.BlockSpec(memory_space=pltpu.VMEM)),
         scratch_shapes=[

time: 66.6 us -> 67 us (level)
  local copies, waits for them, and re-layouts: 0 us -> 1.58 us
  Pallas kernels: 65.9 us -> 64.4 us
    unnamed x0 -> x4, local copies, waits for them, and re-layouts: none -> 1.58 us
    pallas_call x1, Pallas kernels: 63.3 us -> 61.8 us  [body(): pl.pallas_call(kernel, out_shape=(pltpu.VMEM((8, FEAT), BF16), pltpu.VMEM...]
where the time goes in v4:
time: 67 us; the launch traced here: 66.6 us
  Pallas kernels  64.4 us (96%)
  local copies, waits for them, and re-layouts  1.58 us (2%)
    pallas_call x1, Pallas kernels, body(): pl.pallas_call(kernel, out_shape=(pltpu.VMEM((8, FEAT), BF16), pltpu.VMEM...  61.8 us
    pallas_call x1, Pallas kernels, body(): pl.pallas_call(finish, out_shape=(jax.ShapeDtypeStruct((8, FEAT), BF16),...  2.56 us
    unnamed x4, local copies, waits for them, and re-layouts  1.58 us

profile of v4, /device:TPU:1, one launch (start us, length us, event | category | flops | bytes accessed | tf_op | source)
XLA Modules:
  0.0 66.6 jit_solution(4950635088398685098)
XLA Ops:
  0.6 61.8 %shard_map.113 = (bf16[8,3072]{1,0:T(8,128)(2,1)S(1)}, f32[1024,256]{1,0:T(8,128)S(1)}) custom-call(bf16[128,2048]{1,0:T(8,128)(2,1)} %acts_hbm.1, bf16[128,7168]{1,0:T(8,128)(2,1)} %gate_hbm.1, bf16[128,7168]{1,0:T(8,128)(2,1)} %up_hbm.1, bf16[128,7168]{1,0:T(8,128)(2,1)} %cot_hbm.1, bf16[128,2048]{1,0:T(8,128)(2,1)} %outc_hbm.1, bf16[64,2048]{1,0:T(8,128)(2,1)} %pm_hbm.1, ...), custom_call_target="tpu_custom_call" | custom-call | tf_op jit(solution)/shard_map/pallas_call | solution.py:483
  62.5 0.0 copy-start
  62.5 1.0 %copy-done = f32[1024,256]{1,0:T(8,128)} copy-done((f32[1024,256]{1,0:T(8,128)}, f32[1024,256]{1,0:T(8,128)S(1)}, u32[]{:S(2)}) %copy-start) | copy-done | bytes 1048600
  63.4 0.0 copy-start.1
  63.4 0.6 copy-done.1
  64.0 2.6 %shard_map.114 = (bf16[8,3072]{1,0:T(8,128)(2,1)}, f32[256,1024]{1,0:T(8,128)}) custom-call(bf16[8,3072]{1,0:T(8,128)(2,1)} %copy-done.1, f32[1024,256]{1,0:T(8,128)} %copy-done), custom_call_target="tpu_custom_call" | custom-call | tf_op jit(solution)/shard_map/pallas_call | solution.py:504
Async XLA Ops:
  62.5 1.0 %copy-start = (f32[1024,256]{1,0:T(8,128)}, f32[1024,256]{1,0:T(8,128)S(1)}, u32[]{:S(2)}) copy-start(f32[1024,256]{1,0:T(8,128)S(1)} %get-tuple-element.5.turned_ref) | copy-start | bytes 3145732
  63.4 0.6 copy-start.1
